TPU v7x, 1024 devices: a whole 4x8x16 slice. The times are simulated.
1024 devices in a mesh: row: 16 (over z), col: 64 (over y, x, core).
Axes of the slice: x: 4, y: 8, z: 16, core: 2. Of those that a mesh axis runs over, the one named last changes fastest.
Arguments:
- densities: bfloat16 [16384, 32, 256], P(('row', 'col')), may hold values from -6 to 6
- points: bfloat16 [16384, 3, 256], P(('row', 'col')), may hold values from 0 to 1
- normals: bfloat16 [16384, 3, 256], P(('row', 'col')), may hold values from -1.1953125 to 1.1953125
- source_basis: bfloat16 [16384, 64, 256], P(('row', 'col')), may hold values from -0.375 to 0.375
- target_basis: bfloat16 [16384, 64, 256], P(('row', 'col')), may hold values from -0.75 to 0.75
- upward: bfloat16 [16384, 64, 64], P(('row', 'col')), may hold values from -0.1875 to 0.1875
- downward: bfloat16 [16384, 64, 64], P(('row', 'col')), may hold values from -0.75 to 0.75
- couplings: bfloat16 [16384, 8, 64, 64], P(('row', 'col')), may hold values from -0.25 to 0.25
- coarse_couplings: bfloat16 [16, 64, 4, 64, 64], P('row', 'col'), may hold values from -0.1875 to 0.1875
- near_list: int32 [16384, 12], P(('row', 'col')), may hold values from 0 to 47, as said below
- far_want: int32 [16, 64, 64, 2], P('row', 'col'), may hold values from 0 to 15, as said below
- far_list: int32 [16384, 8], P(('row', 'col')), may hold values from 0 to 127, as said below
- far_count: int32 [16384], P(('row', 'col')), may hold values from 4 to 8
Outputs:
- potentials: float32 [16384, 32, 256], P(('row', 'col'))
Inputs may be any that keep to these rules, and one draw needn't show every extreme that they name: `near_list`: entry 0 of leaf i is 16 + i mod 16; the entries of one leaf are distinct. `far_want`: the 2 entries of one [g, c, p] are distinct. `far_list`: on each device every value appears exactly 16 * 8 / 128 times.
All inputs are finite; a program needn't handle non-finite values.
Results may differ from a plain program's by a relative error of at most 0.0029.
Values may be sent and summed in bfloat16 or wider, within the bound.
A program may use at most 32 MiB of HBM per device.

v0:
```python
import math

import jax
import jax.numpy as jnp
from jax import lax
from jax.sharding import PartitionSpec as P

soften_square = 0.0025
kernel_scale = 0.25 / math.pi


def extended(block, sides, width):
    for axis, dim in sides:
        count = lax.axis_size(axis)
        forward = [(i, i + 1) for i in range(count - 1)]
        forward.append((count - 1, 0))
        backward = [(target, source) for source, target in forward]
        low = lax.ppermute(
            lax.slice_in_dim(block, block.shape[dim] - width, None, axis=dim), axis, forward
        )
        high = lax.ppermute(lax.slice_in_dim(block, 0, width, axis=dim), axis, backward)
        block = jnp.concatenate([low, block, high], axis=dim)
    return block


def partner_2(block, axis, stride):
    count = lax.axis_size(axis)
    route = []
    for low in range(count):
        high = low | 1 << stride
        if high != low and high < count:
            route += [(low, high), (high, low)]
    return lax.ppermute(block, axis, route)


def near_tile(target_points, source_points, source_normals):
    target = target_points.astype(jnp.float32)
    source = source_points.astype(jnp.float32)
    normal = source_normals.astype(jnp.float32)
    delta_x = target[0][None, None, :] - source[:, 0, :, None]
    delta_y = target[1][None, None, :] - source[:, 1, :, None]
    delta_z = target[2][None, None, :] - source[:, 2, :, None]
    squared = delta_x * delta_x + delta_y * delta_y + delta_z * delta_z + soften_square
    normal_dot = (
        normal[:, 0, :, None] * delta_x
        + normal[:, 1, :, None] * delta_y
        + normal[:, 2, :, None] * delta_z
    )
    return (kernel_scale * normal_dot * lax.rsqrt(squared) / squared).astype(jnp.bfloat16)


def local(
    densities,
    points,
    normals,
    source_basis,
    target_basis,
    upward,
    downward,
    couplings,
    coarse_couplings,
    near_list,
    far_want,
    far_list,
    far_count,
):
    leaf_count = densities.shape[0]
    rhs_count = densities.shape[1]
    rank_size = source_basis.shape[1]
    entry_count = far_list.shape[1]
    slot_count = far_want.shape[3]
    peer_count = lax.axis_size("col")
    skeleton = jnp.einsum(
        "lrq,lmq->lrm", densities, source_basis, preferred_element_type=jnp.float32
    ).astype(jnp.bfloat16)
    stacked = jnp.concatenate((densities, points, normals), axis=1)
    padded = extended(stacked, (("col", 0),), leaf_count)

    def near_leaf(inputs):
        target_points, source_ids = inputs
        sources = jnp.take(padded, source_ids, axis=0)
        kernel_tile = near_tile(
            target_points, sources[:, rhs_count : rhs_count + 3], sources[:, rhs_count + 3 :]
        )
        return jnp.einsum(
            "krq,kqp->rp", sources[:, :rhs_count], kernel_tile, preferred_element_type=jnp.float32
        )

    near_part = lax.map(near_leaf, (points, near_list))
    skeleton_rows = skeleton.reshape(leaf_count, rhs_count * rank_size)
    requested = lax.all_to_all(far_want, "col", split_axis=2, concat_axis=2, tiled=True)
    outgoing = jnp.take(skeleton_rows, requested.reshape(-1), axis=0)
    outgoing = outgoing.reshape(peer_count, slot_count, rhs_count * rank_size)
    received = lax.all_to_all(outgoing, "col", split_axis=0, concat_axis=0, tiled=True)
    received = received.reshape(peer_count * slot_count, rhs_count * rank_size)
    chosen = jnp.take(received, far_list.reshape(-1), axis=0).reshape(
        leaf_count, entry_count, rhs_count, rank_size
    )
    active = jnp.arange(entry_count, dtype=jnp.int32)[None, :] < far_count[:, None]
    chosen = jnp.where(active[:, :, None, None], chosen, jnp.zeros_like(chosen))
    far_coeff = jnp.einsum("lkrm,lkmn->lrn", chosen, couplings, preferred_element_type=jnp.float32)
    device_sum = jnp.einsum("lrm,lmn->rn", skeleton, upward, preferred_element_type=jnp.float32)
    levels = lax.axis_size("row").bit_length() - 1
    coarse_mix = coarse_couplings.reshape(levels, rank_size, rank_size).astype(jnp.float32)
    coarse_sum = jnp.zeros((rhs_count, rank_size), jnp.float32)
    combined = device_sum
    for level in range(levels):
        partner = partner_2(combined, "row", level)
        coarse_sum = coarse_sum + jnp.dot(
            partner, coarse_mix[level], precision=lax.Precision.HIGHEST
        )
        combined = combined + partner
    coarse_field = coarse_sum.astype(jnp.bfloat16)
    leaf_coeff = (
        far_coeff
        + jnp.einsum("rm,lmn->lrn", coarse_field, downward, preferred_element_type=jnp.float32)
    ).astype(jnp.bfloat16)
    far_part = jnp.einsum(
        "lrm,lmq->lrq", leaf_coeff, target_basis, preferred_element_type=jnp.float32
    )
    return near_part + far_part


def solution(mesh):
    placed = (
        P(("row", "col"), None, None),
        P(("row", "col"), None, None),
        P(("row", "col"), None, None),
        P(("row", "col"), None, None),
        P(("row", "col"), None, None),
        P(("row", "col"), None, None),
        P(("row", "col"), None, None),
        P(("row", "col"), None, None, None),
        P("row", "col", None, None, None),
        P(("row", "col"), None),
        P("row", "col", None, None),
        P(("row", "col"), None),
        P(("row", "col")),
    )
    return jax.shard_map(
        local, mesh=mesh, in_specs=placed, out_specs=P(("row", "col"), None, None), check_vma=False
    )
```

profile of v0, /device:TPU:1, one launch (start us, length us, event | category | flops | bytes accessed | tf_op | source)
XLA Modules:
  0.0 190.2 jit_solution(4228000980563131757)
XLA Ops:
  2.7 16.1 %collective-permute-start.1 = (bf16[16,38,256]{2,1,0:T(8,128)(2,1)S(1)}, bf16[16,38,256]{2,1,0:T(8,128)(2,1)}, u32[]{:S(2)}, u32[]{:S(2)}) collective-permute-start(bf16[16,38,256]{2,1,0:T(8,128)(2,1)S(1)} %pad_maximum_fusion.1), channel_id=1, source_target_pairs={{1,0},{2,1},{3,2},{4,3},{5,4},{6,5},{7,6},{8,7},{9,8},{10,9},{11,1... | collective-permute-start | bytes 933896 | tf_op jit(solution)/shard_map/ppermute | solution.py:21
  22.1 6.9 %all-to-all-start = ((s32[1,1,64,2]{3,1,0,2:T(1,128)}), s32[1,1,64,2]{3,1,0,2:T(1,128)S(1)}, u32[]{:S(2)}, u32[]{:S(2)}) async-start(s32[1,1,64,2]{3,1,0,2:T(1,128)} %copy.29), calls=%async_computation | async-start | bytes 65536 | tf_op jit(solution)/shard_map/all_to_all | solution.py:91
  34.0 4.3 %all-to-all-done = s32[1,1,64,2]{3,1,0,2:T(1,128)S(1)} async-done(((s32[1,1,64,2]{3,1,0,2:T(1,128)}), s32[1,1,64,2]{3,1,0,2:T(1,128)S(1)}, u32[]{:S(2)}, u32[]{:S(2)}) %all-to-all-start) | async-done | bytes 544 | tf_op jit(solution)/shard_map/all_to_all | solution.py:91
  46.5 6.3 %all-to-all-start.1 = ((bf16[64,2,2048]{2,1,0:T(2,128)(2,1)}), bf16[64,2,2048]{2,1,0:T(2,128)(2,1)}, u32[]{:S(2)}, u32[]{:S(2)}) async-start(bf16[64,2,2048]{2,1,0:T(2,128)(2,1)} %broadcast_select_fusion.1), calls=%async_computation.1 | async-start | bytes 1048576 | tf_op jit(solution)/shard_map/all_to_all | solution.py:94
  52.8 10.6 %collective-permute-start.4 = (f32[32,64]{1,0:T(8,128)S(1)}, f32[32,64]{1,0:T(8,128)S(1)}, u32[]{:S(2)}, u32[]{:S(2)}) collective-permute-start(f32[32,64]{1,0:T(8,128)S(1)} %add.111), channel_id=1, source_target_pairs={{0,256},{256,0},{64,320},{320,64},{128,384},{384,128},{192,448},{4... | collective-permute-start | bytes 24584 | tf_op jit(solution)/shard_map/ppermute | solution.py:33
  65.0 13.4 %collective-permute-start.5 = (f32[32,64]{1,0:T(8,128)S(1)}, f32[32,64]{1,0:T(8,128)S(1)}, u32[]{:S(2)}, u32[]{:S(2)}) collective-permute-start(f32[32,64]{1,0:T(8,128)S(1)} %add.113), channel_id=1, source_target_pairs={{0,512},{512,0},{64,576},{576,64},{128,640},{640,128},{192,704},{7... | collective-permute-start | bytes 24584 | tf_op jit(solution)/shard_map/ppermute | solution.py:33
  81.0 99.0 %while.10 = (s32[]{:T(128)}, f32[16,32,256]{2,1,0:T(8,128)}, s32[16,12]{1,0:T(8,128)}, bf16[48,38,256]{2,1,0:T(8,128)(2,1)S(1)}, bf16[16,3,256]{2,0,1:T(8,128)(2,1)}, /*index=5*/s32[]{:T(128)}) while((s32[]{:T(128)}, f32[16,32,256]{2,1,0:T(8,128)}, s32[16,12]{1,0:T(8,128)}, bf16[48,38,256]{2,1,0:T(8,128)(2,1)S(1)}, ...), condition=%wide.region_1.2_spmd, body=%wide.region_0.1_spmd.sunk | while | flops 64624492 | bytes 1685349 | solution.py:89
  83.9 3.2 %fusion.75 = f32[16,32,256]{2,1,0:T(8,128)} fusion(f32[16,32,256]{2,1,0:T(8,128)} %get-tuple-element.117, s32[]{:T(128)S(6)} %copy.67, f32[12,256]{1,0:T(8,128)S(1)} %bitcast.104, f32[256]{0:T(256)S(1)} %bitcast.111, f32[12,256]{1,0:T(8,128)S(1)} %bitcast.105, f32[12,256]{1,0:T(8,128)S(1)} %bitcast.106, f32[256]{0:T(256)S(1)} %bitcast.112, ...), kind=kOutput, calls=%fused_computation.20.clone.1 | convolution fusion | flops 64487424 | bytes 330756 | tf_op jit(solution)/shard_map/while/body/eval_jaxpr/krq,kqp->rp/dot_general | solution.py:85
  90.1 3.2 %fusion.75 = f32[16,32,256]{2,1,0:T(8,128)} fusion(f32[16,32,256]{2,1,0:T(8,128)} %get-tuple-element.117, s32[]{:T(128)S(6)} %copy.67, f32[12,256]{1,0:T(8,128)S(1)} %bitcast.104, f32[256]{0:T(256)S(1)} %bitcast.111, f32[12,256]{1,0:T(8,128)S(1)} %bitcast.105, f32[12,256]{1,0:T(8,128)S(1)} %bitcast.106, f32[256]{0:T(256)S(1)} %bitcast.112, ...), kind=kOutput, calls=%fused_computation.20.clone.1 | convolution fusion | flops 64487424 | bytes 330756 | tf_op jit(solution)/shard_map/while/body/eval_jaxpr/krq,kqp->rp/dot_general | solution.py:85
  96.3 3.2 %fusion.75 = f32[16,32,256]{2,1,0:T(8,128)} fusion(f32[16,32,256]{2,1,0:T(8,128)} %get-tuple-element.117, s32[]{:T(128)S(6)} %copy.67, f32[12,256]{1,0:T(8,128)S(1)} %bitcast.104, f32[256]{0:T(256)S(1)} %bitcast.111, f32[12,256]{1,0:T(8,128)S(1)} %bitcast.105, f32[12,256]{1,0:T(8,128)S(1)} %bitcast.106, f32[256]{0:T(256)S(1)} %bitcast.112, ...), kind=kOutput, calls=%fused_computation.20.clone.1 | convolution fusion | flops 64487424 | bytes 330756 | tf_op jit(solution)/shard_map/while/body/eval_jaxpr/krq,kqp->rp/dot_general | solution.py:85
  102.5 3.2 %fusion.75 = f32[16,32,256]{2,1,0:T(8,128)} fusion(f32[16,32,256]{2,1,0:T(8,128)} %get-tuple-element.117, s32[]{:T(128)S(6)} %copy.67, f32[12,256]{1,0:T(8,128)S(1)} %bitcast.104, f32[256]{0:T(256)S(1)} %bitcast.111, f32[12,256]{1,0:T(8,128)S(1)} %bitcast.105, f32[12,256]{1,0:T(8,128)S(1)} %bitcast.106, f32[256]{0:T(256)S(1)} %bitcast.112, ...), kind=kOutput, calls=%fused_computation.20.clone.1 | convolution fusion | flops 64487424 | bytes 330756 | tf_op jit(solution)/shard_map/while/body/eval_jaxpr/krq,kqp->rp/dot_general | solution.py:85
  108.7 3.2 %fusion.75 = f32[16,32,256]{2,1,0:T(8,128)} fusion(f32[16,32,256]{2,1,0:T(8,128)} %get-tuple-element.117, s32[]{:T(128)S(6)} %copy.67, f32[12,256]{1,0:T(8,128)S(1)} %bitcast.104, f32[256]{0:T(256)S(1)} %bitcast.111, f32[12,256]{1,0:T(8,128)S(1)} %bitcast.105, f32[12,256]{1,0:T(8,128)S(1)} %bitcast.106, f32[256]{0:T(256)S(1)} %bitcast.112, ...), kind=kOutput, calls=%fused_computation.20.clone.1 | convolution fusion | flops 64487424 | bytes 330756 | tf_op jit(solution)/shard_map/while/body/eval_jaxpr/krq,kqp->rp/dot_general | solution.py:85
  114.9 3.2 %fusion.75 = f32[16,32,256]{2,1,0:T(8,128)} fusion(f32[16,32,256]{2,1,0:T(8,128)} %get-tuple-element.117, s32[]{:T(128)S(6)} %copy.67, f32[12,256]{1,0:T(8,128)S(1)} %bitcast.104, f32[256]{0:T(256)S(1)} %bitcast.111, f32[12,256]{1,0:T(8,128)S(1)} %bitcast.105, f32[12,256]{1,0:T(8,128)S(1)} %bitcast.106, f32[256]{0:T(256)S(1)} %bitcast.112, ...), kind=kOutput, calls=%fused_computation.20.clone.1 | convolution fusion | flops 64487424 | bytes 330756 | tf_op jit(solution)/shard_map/while/body/eval_jaxpr/krq,kqp->rp/dot_general | solution.py:85
  121.1 3.2 %fusion.75 = f32[16,32,256]{2,1,0:T(8,128)} fusion(f32[16,32,256]{2,1,0:T(8,128)} %get-tuple-element.117, s32[]{:T(128)S(6)} %copy.67, f32[12,256]{1,0:T(8,128)S(1)} %bitcast.104, f32[256]{0:T(256)S(1)} %bitcast.111, f32[12,256]{1,0:T(8,128)S(1)} %bitcast.105, f32[12,256]{1,0:T(8,128)S(1)} %bitcast.106, f32[256]{0:T(256)S(1)} %bitcast.112, ...), kind=kOutput, calls=%fused_computation.20.clone.1 | convolution fusion | flops 64487424 | bytes 330756 | tf_op jit(solution)/shard_map/while/body/eval_jaxpr/krq,kqp->rp/dot_general | solution.py:85
  127.3 3.2 %fusion.75 = f32[16,32,256]{2,1,0:T(8,128)} fusion(f32[16,32,256]{2,1,0:T(8,128)} %get-tuple-element.117, s32[]{:T(128)S(6)} %copy.67, f32[12,256]{1,0:T(8,128)S(1)} %bitcast.104, f32[256]{0:T(256)S(1)} %bitcast.111, f32[12,256]{1,0:T(8,128)S(1)} %bitcast.105, f32[12,256]{1,0:T(8,128)S(1)} %bitcast.106, f32[256]{0:T(256)S(1)} %bitcast.112, ...), kind=kOutput, calls=%fused_computation.20.clone.1 | convolution fusion | flops 64487424 | bytes 330756 | tf_op jit(solution)/shard_map/while/body/eval_jaxpr/krq,kqp->rp/dot_general | solution.py:85
  133.5 3.2 %fusion.75 = f32[16,32,256]{2,1,0:T(8,128)} fusion(f32[16,32,256]{2,1,0:T(8,128)} %get-tuple-element.117, s32[]{:T(128)S(6)} %copy.67, f32[12,256]{1,0:T(8,128)S(1)} %bitcast.104, f32[256]{0:T(256)S(1)} %bitcast.111, f32[12,256]{1,0:T(8,128)S(1)} %bitcast.105, f32[12,256]{1,0:T(8,128)S(1)} %bitcast.106, f32[256]{0:T(256)S(1)} %bitcast.112, ...), kind=kOutput, calls=%fused_computation.20.clone.1 | convolution fusion | flops 64487424 | bytes 330756 | tf_op jit(solution)/shard_map/while/body/eval_jaxpr/krq,kqp->rp/dot_general | solution.py:85
  139.7 3.2 %fusion.75 = f32[16,32,256]{2,1,0:T(8,128)} fusion(f32[16,32,256]{2,1,0:T(8,128)} %get-tuple-element.117, s32[]{:T(128)S(6)} %copy.67, f32[12,256]{1,0:T(8,128)S(1)} %bitcast.104, f32[256]{0:T(256)S(1)} %bitcast.111, f32[12,256]{1,0:T(8,128)S(1)} %bitcast.105, f32[12,256]{1,0:T(8,128)S(1)} %bitcast.106, f32[256]{0:T(256)S(1)} %bitcast.112, ...), kind=kOutput, calls=%fused_computation.20.clone.1 | convolution fusion | flops 64487424 | bytes 330756 | tf_op jit(solution)/shard_map/while/body/eval_jaxpr/krq,kqp->rp/dot_general | solution.py:85
  145.8 3.2 %fusion.75 = f32[16,32,256]{2,1,0:T(8,128)} fusion(f32[16,32,256]{2,1,0:T(8,128)} %get-tuple-element.117, s32[]{:T(128)S(6)} %copy.67, f32[12,256]{1,0:T(8,128)S(1)} %bitcast.104, f32[256]{0:T(256)S(1)} %bitcast.111, f32[12,256]{1,0:T(8,128)S(1)} %bitcast.105, f32[12,256]{1,0:T(8,128)S(1)} %bitcast.106, f32[256]{0:T(256)S(1)} %bitcast.112, ...), kind=kOutput, calls=%fused_computation.20.clone.1 | convolution fusion | flops 64487424 | bytes 330756 | tf_op jit(solution)/shard_map/while/body/eval_jaxpr/krq,kqp->rp/dot_general | solution.py:85
  152.0 3.2 %fusion.75 = f32[16,32,256]{2,1,0:T(8,128)} fusion(f32[16,32,256]{2,1,0:T(8,128)} %get-tuple-element.117, s32[]{:T(128)S(6)} %copy.67, f32[12,256]{1,0:T(8,128)S(1)} %bitcast.104, f32[256]{0:T(256)S(1)} %bitcast.111, f32[12,256]{1,0:T(8,128)S(1)} %bitcast.105, f32[12,256]{1,0:T(8,128)S(1)} %bitcast.106, f32[256]{0:T(256)S(1)} %bitcast.112, ...), kind=kOutput, calls=%fused_computation.20.clone.1 | convolution fusion | flops 64487424 | bytes 330756 | tf_op jit(solution)/shard_map/while/body/eval_jaxpr/krq,kqp->rp/dot_general | solution.py:85
  158.2 3.2 %fusion.75 = f32[16,32,256]{2,1,0:T(8,128)} fusion(f32[16,32,256]{2,1,0:T(8,128)} %get-tuple-element.117, s32[]{:T(128)S(6)} %copy.67, f32[12,256]{1,0:T(8,128)S(1)} %bitcast.104, f32[256]{0:T(256)S(1)} %bitcast.111, f32[12,256]{1,0:T(8,128)S(1)} %bitcast.105, f32[12,256]{1,0:T(8,128)S(1)} %bitcast.106, f32[256]{0:T(256)S(1)} %bitcast.112, ...), kind=kOutput, calls=%fused_computation.20.clone.1 | convolution fusion | flops 64487424 | bytes 330756 | tf_op jit(solution)/shard_map/while/body/eval_jaxpr/krq,kqp->rp/dot_general | solution.py:85
  164.4 3.2 %fusion.75 = f32[16,32,256]{2,1,0:T(8,128)} fusion(f32[16,32,256]{2,1,0:T(8,128)} %get-tuple-element.117, s32[]{:T(128)S(6)} %copy.67, f32[12,256]{1,0:T(8,128)S(1)} %bitcast.104, f32[256]{0:T(256)S(1)} %bitcast.111, f32[12,256]{1,0:T(8,128)S(1)} %bitcast.105, f32[12,256]{1,0:T(8,128)S(1)} %bitcast.106, f32[256]{0:T(256)S(1)} %bitcast.112, ...), kind=kOutput, calls=%fused_computation.20.clone.1 | convolution fusion | flops 64487424 | bytes 330756 | tf_op jit(solution)/shard_map/while/body/eval_jaxpr/krq,kqp->rp/dot_general | solution.py:85
  170.6 3.2 %fusion.75 = f32[16,32,256]{2,1,0:T(8,128)} fusion(f32[16,32,256]{2,1,0:T(8,128)} %get-tuple-element.117, s32[]{:T(128)S(6)} %copy.67, f32[12,256]{1,0:T(8,128)S(1)} %bitcast.104, f32[256]{0:T(256)S(1)} %bitcast.111, f32[12,256]{1,0:T(8,128)S(1)} %bitcast.105, f32[12,256]{1,0:T(8,128)S(1)} %bitcast.106, f32[256]{0:T(256)S(1)} %bitcast.112, ...), kind=kOutput, calls=%fused_computation.20.clone.1 | convolution fusion | flops 64487424 | bytes 330756 | tf_op jit(solution)/shard_map/while/body/eval_jaxpr/krq,kqp->rp/dot_general | solution.py:85
  176.8 3.2 %fusion.75 = f32[16,32,256]{2,1,0:T(8,128)} fusion(f32[16,32,256]{2,1,0:T(8,128)} %get-tuple-element.117, s32[]{:T(128)S(6)} %copy.67, f32[12,256]{1,0:T(8,128)S(1)} %bitcast.104, f32[256]{0:T(256)S(1)} %bitcast.111, f32[12,256]{1,0:T(8,128)S(1)} %bitcast.105, f32[12,256]{1,0:T(8,128)S(1)} %bitcast.106, f32[256]{0:T(256)S(1)} %bitcast.112, ...), kind=kOutput, calls=%fused_computation.20.clone.1 | convolution fusion | flops 64487424 | bytes 330756 | tf_op jit(solution)/shard_map/while/body/eval_jaxpr/krq,kqp->rp/dot_general | solution.py:85
  184.3 2.7 %convolution_bitcast_fusion.1 = f32[16,32,64]{2,1,0:T(8,128)} fusion(bf16[16,8,64,64]{3,2,1,0:T(8,128)(2,1)S(1)} %copy-done, bf16[16,8,32,64]{3,2,1,0:T(8,128)(2,1)} %gather.19, pred[16,8]{1,0:T(8,128)(4,1)S(1)} %copy.28, pred[16,8]{1,0:T(8,128)(4,1)S(1)} %iota_compare_fusion), kind=kOutput, calls=%fused_computation.42 | convolution fusion | flops 34078720 | bytes 1704192 | tf_op jit(solution)/shard_map/lkrm,lkmn->lrn/dot_general | solution.py:101
  (303 shorter events, 76.5 us)
Async XLA Ops:
  0.0 184.3 %copy-start = (bf16[16,8,64,64]{3,2,1,0:T(8,128)(2,1)S(1)}, bf16[16,8,64,64]{3,2,1,0:T(8,128)(2,1)}, u32[]{:S(2)}) copy-start(bf16[16,8,64,64]{3,2,1,0:T(8,128)(2,1)} %param.22) | copy-start | bytes 3145732
  0.0 33.4 %copy-start.5 = (s32[16,8]{0,1:T(8,128)S(1)}, s32[16,8]{0,1:T(8,128)}, u32[]{:S(2)}) copy-start(s32[16,8]{0,1:T(8,128)} %param.26) | copy-start | bytes 1540
  0.0 33.6 %copy-start.6 = (s32[16]{0:T(128)S(1)}, s32[16]{0:T(128)}, u32[]{:S(2)}) copy-start(s32[16]{0:T(128)} %param.27) | copy-start | bytes 196
  2.7 77.1 %collective-permute-start.1 = (bf16[16,38,256]{2,1,0:T(8,128)(2,1)S(1)}, bf16[16,38,256]{2,1,0:T(8,128)(2,1)}, u32[]{:S(2)}, u32[]{:S(2)}) collective-permute-start(bf16[16,38,256]{2,1,0:T(8,128)(2,1)S(1)} %pad_maximum_fusion.1), channel_id=1, source_target_pairs={{1,0},{2,1},{3,2},{4,3},{5,4},{6,5},{7,6},{8,7},{9,8},{10,9},{11,1... | collective-permute-start | bytes 933896 | tf_op jit(solution)/shard_map/ppermute | solution.py:21
  18.7 61.1 %collective-permute-start = (bf16[16,38,256]{2,1,0:T(8,128)(2,1)S(1)}, bf16[16,38,256]{2,1,0:T(8,128)(2,1)}, u32[]{:S(2)}, u32[]{:S(2)}) collective-permute-start(bf16[16,38,256]{2,1,0:T(8,128)(2,1)S(1)} %pad_maximum_fusion.1), channel_id=1, source_target_pairs={{0,1},{1,2},{2,3},{3,4},{4,5},{5,6},{6,7},{7,8},{8,9},{9,10},{10,1... | collective-permute-start | bytes 933896 | tf_op jit(solution)/shard_map/ppermute | solution.py:18
  22.1 16.3 %all-to-all-start = ((s32[1,1,64,2]{3,1,0,2:T(1,128)}), s32[1,1,64,2]{3,1,0,2:T(1,128)S(1)}, u32[]{:S(2)}, u32[]{:S(2)}) async-start(s32[1,1,64,2]{3,1,0,2:T(1,128)} %copy.29), calls=%async_computation | async-start | bytes 65536 | tf_op jit(solution)/shard_map/all_to_all | solution.py:91
  31.5 10.7 %collective-permute-start.2 = (f32[32,64]{1,0:T(8,128)S(1)}, f32[32,64]{1,0:T(8,128)S(1)}, u32[]{:S(2)}, u32[]{:S(2)}) collective-permute-start(f32[32,64]{1,0:T(8,128)S(1)} %convolution_bitcast_fusion.2), channel_id=1, source_target_pairs={{0,64},{64,0},{128,192},{192,128},{256,320},{320,256},{384,448},{4... | collective-permute-start | bytes 24584 | tf_op jit(solution)/shard_map/ppermute | solution.py:33
  40.9 22.6 %copy-start.4 = (bf16[1,1,4,64,64]{4,3,2,1,0:T(8,128)(2,1)S(1)}, bf16[1,1,4,64,64]{4,3,2,1,0:T(8,128)(2,1)}, u32[]{:S(2)}) copy-start(bf16[1,1,4,64,64]{4,3,2,1,0:T(8,128)(2,1)} %param.23) | copy-start | bytes 98308
  40.9 38.9 %copy-start.1 = (bf16[16,32,256]{2,1,0:T(8,128)(2,1)S(1)}, bf16[16,32,256]{2,1,0:T(8,128)(2,1)}, u32[]{:S(2)}) copy-start(bf16[16,32,256]{2,1,0:T(8,128)(2,1)} %param.15) | copy-start | bytes 786436
  42.2 10.6 %collective-permute-start.3 = (f32[32,64]{1,0:T(8,128)S(1)}, f32[32,64]{1,0:T(8,128)S(1)}, u32[]{:S(2)}, u32[]{:S(2)}) collective-permute-start(f32[32,64]{1,0:T(8,128)S(1)} %add.109), channel_id=1, source_target_pairs={{0,128},{128,0},{64,192},{192,64},{256,384},{384,256},{320,448},{4... | collective-permute-start | bytes 24584 | tf_op jit(solution)/shard_map/ppermute | solution.py:33
  46.5 133.5 %all-to-all-start.1 = ((bf16[64,2,2048]{2,1,0:T(2,128)(2,1)}), bf16[64,2,2048]{2,1,0:T(2,128)(2,1)}, u32[]{:S(2)}, u32[]{:S(2)}) async-start(bf16[64,2,2048]{2,1,0:T(2,128)(2,1)} %broadcast_select_fusion.1), calls=%async_computation.1 | async-start | bytes 1048576 | tf_op jit(solution)/shard_map/all_to_all | solution.py:94
  52.8 12.2 %collective-permute-start.4 = (f32[32,64]{1,0:T(8,128)S(1)}, f32[32,64]{1,0:T(8,128)S(1)}, u32[]{:S(2)}, u32[]{:S(2)}) collective-permute-start(f32[32,64]{1,0:T(8,128)S(1)} %add.111), channel_id=1, source_target_pairs={{0,256},{256,0},{64,320},{320,64},{128,384},{384,128},{192,448},{4... | collective-permute-start | bytes 24584 | tf_op jit(solution)/shard_map/ppermute | solution.py:33
  65.0 14.5 %collective-permute-start.5 = (f32[32,64]{1,0:T(8,128)S(1)}, f32[32,64]{1,0:T(8,128)S(1)}, u32[]{:S(2)}, u32[]{:S(2)}) collective-permute-start(f32[32,64]{1,0:T(8,128)S(1)} %add.113), channel_id=1, source_target_pairs={{0,512},{512,0},{64,576},{576,64},{128,640},{640,128},{192,704},{7... | collective-permute-start | bytes 24584 | tf_op jit(solution)/shard_map/ppermute | solution.py:33
  184.3 2.7 %copy-start.2 = (bf16[16,64,256]{2,1,0:T(8,128)(2,1)S(1)}, bf16[16,64,256]{2,1,0:T(8,128)(2,1)}, u32[]{:S(2)}) copy-start(bf16[16,64,256]{2,1,0:T(8,128)(2,1)} %param.19) | copy-start | bytes 1572868
  184.3 2.7 %copy-start.3 = (bf16[16,64,64]{2,1,0:T(8,128)(2,1)S(1)}, bf16[16,64,64]{2,1,0:T(8,128)(2,1)}, u32[]{:S(2)}) copy-start(bf16[16,64,64]{2,1,0:T(8,128)(2,1)} %param.21) | copy-start | bytes 393220
where the time goes:
time: 193 us; the launch traced here: 190 us
  starting transfers between devices  59 us (31%)
  matrix products  59 us (31%)
  other arithmetic  43.1 us (22%)
  local copies, waits for them, and re-layouts  20.9 us (11%)
  waiting for transfers between devices  6.73 us (3%)
    dot_general x16, matrix products, near_leaf(): jnp.einsum('krq,kqp->rp', sources[:, :rhs_count], kernel_tile, preferred_...  51.9 us
    ppermute x4, starting transfers between devices, partner_2(): return lax.ppermute(block, axis, route)  27.9 us
    ppermute x1, starting transfers between devices, extended(): lax.ppermute(lax.slice_in_dim(block, 0, width, axis=dim), axis, backward)  16.1 us
    select_n x32, other arithmetic, near_leaf(): sources = jnp.take(padded, source_ids, axis=0)  12.5 us
    convert_element_type x16, other arithmetic, near_tile(): target = target_points.astype(jnp.float32)  11.5 us
    and x16, other arithmetic, near_leaf(): sources = jnp.take(padded, source_ids, axis=0)  11.3 us
    gather x16, local copies, waits for them, and re-layouts, near_leaf(): sources = jnp.take(padded, source_ids, axis=0)  9 us
    all_to_all x1, starting transfers between devices, local(): lax.all_to_all(far_want, 'col', split_axis=2, concat_axis=2, tiled=True)  6.9 us
  transfers between devices with their start and end apart: 8, of which 3 were waited for; matrix products, arithmetic and copies ran while one was open for 58% of the time, Pallas kernels for 0%

commit v1 on v0

v1 whole, which is shorter than its diff:
```python
import math

import jax
import jax.numpy as jnp
from jax import lax
from jax.experimental import pallas as pl
from jax.experimental.pallas import tpu as pltpu
from jax.sharding import PartitionSpec as P

soften_square = 0.0025
kernel_scale = 0.25 / math.pi

LEAVES = 16
RHS = 32
RANK = 64
LEAF = 256
NEAR = 12
FAR = 8
SLOTS = 2
LEVELS = 4
ROWS = 16
COLS = 64
DEPTH = 16
VECTOR_ROWS = 192

f32 = jnp.float32
bf16 = jnp.bfloat16
MESH = pl.DeviceIdType.MESH
CONTRACT_LAST = (((1,), (1,)), ((), ()))


def split3(value):
    high = value.astype(bf16).astype(f32)
    rest = value - high
    middle = rest.astype(bf16).astype(f32)
    return high, middle, rest - middle


def kernel(
    densities, points, normals, source_basis, target_basis, upward, downward, couplings,
    coarse_couplings, near_list, far_want, far_list, far_count,
    out,
    dens, geom, wants_own, wants, asked, sbasis, tbasis, up, down, coup, coarse_coup,
    nlist, flist, fcount, skel, outgoing, received, sums, features, sources, rows, columns, result,
    load_sem, small_sem, halo_send, halo_recv, want_send, want_recv, far_send, far_recv,
    sum_send, sum_recv, out_sem,
):
    g = lax.axis_index("row")
    c = lax.axis_index("col")
    above = lax.rem(c + 1, COLS)
    below = lax.rem(c + COLS - 1, COLS)

    def load(source, target, sem):
        copy = pltpu.make_async_copy(source, target, sem)
        copy.start()
        return copy

    load_points = load(points, geom.at[1, pl.ds(0, 3)], load_sem.at[0])
    load_normals = load(normals, geom.at[1, pl.ds(3, 3)], load_sem.at[1])
    load_dens = load(densities, dens.at[1], load_sem.at[2])
    load_wants = load(far_want, wants_own, load_sem.at[3])
    load_sbasis = load(source_basis, sbasis, load_sem.at[4])
    load_up = load(upward, up, load_sem.at[5])
    load_nlist = load(near_list, nlist, small_sem.at[0])
    load_flist = load(far_list, flist, small_sem.at[1])
    load_fcount = load(far_count, fcount, small_sem.at[2])
    load_coarse = load(coarse_couplings, coarse_coup, load_sem.at[6])
    load_coup = load(couplings, coup, load_sem.at[7])
    load_down = load(downward, down, load_sem.at[8])
    load_tbasis = load(target_basis, tbasis, load_sem.at[9])

    barrier = pltpu.get_barrier_semaphore()

    def greet_col(d, _):
        pl.semaphore_signal(
            barrier, inc=1, device_id=(g, lax.rem(c + d, COLS)), device_id_type=MESH
        )
        return 0

    def greet_row(d, _):
        pl.semaphore_signal(
            barrier, inc=1, device_id=(lax.rem(g + d, ROWS), c), device_id_type=MESH
        )
        return 0

    lax.fori_loop(1, COLS, greet_col, 0)
    lax.fori_loop(1, ROWS, greet_row, 0)

    load_points.wait()
    load_normals.wait()
    load_dens.wait()
    load_wants.wait()
    pl.semaphore_wait(barrier, COLS + ROWS - 2)

    halo = []
    for index, (buffer, slot, target) in enumerate(
        ((geom, 0, above), (geom, 2, below), (dens, 0, above), (dens, 2, below))
    ):
        copy = pltpu.make_async_remote_copy(
            src_ref=buffer.at[1],
            dst_ref=buffer.at[slot],
            send_sem=halo_send.at[index],
            recv_sem=halo_recv.at[index],
            device_id=(g, target),
            device_id_type=MESH,
        )
        copy.start()
        halo.append(copy)

    def send_want(d, _):
        pltpu.make_async_remote_copy(
            src_ref=wants_own,
            dst_ref=wants.at[c],
            send_sem=want_send,
            recv_sem=want_recv,
            device_id=(g, lax.rem(c + d, COLS)),
            device_id_type=MESH,
        ).start()
        return 0

    lax.fori_loop(1, COLS, send_want, 0)

    load_sbasis.wait()
    load_up.wait()

    total = jnp.zeros((RHS, RANK), f32)
    for leaf in range(LEAVES):
        value = lax.dot_general(
            dens[1, leaf], sbasis[leaf], CONTRACT_LAST, preferred_element_type=f32
        )
        rounded = value.astype(bf16)
        value = rounded.astype(f32)
        skel[leaf] = jnp.concatenate([value[:16], value[16:]], axis=1).astype(bf16)
        total = total + jnp.dot(rounded, up[leaf], preferred_element_type=f32)
    sums[g] = jnp.concatenate([total[:16], total[16:]], axis=1)

    def send_sum(d, _):
        pltpu.make_async_remote_copy(
            src_ref=sums.at[g],
            dst_ref=sums.at[g],
            send_sem=sum_send,
            recv_sem=sum_recv,
            device_id=(lax.rem(g + d, ROWS), c),
            device_id_type=MESH,
        ).start()
        return 0

    lax.fori_loop(1, ROWS, send_sum, 0)

    zero = jnp.zeros((LEAVES, LEAF), f32)
    one = jnp.ones((LEAVES, LEAF), f32)

    def put(row, first, second):
        for part, value in enumerate((first, second)):
            for half in range(2):
                features[2 * part + half, pl.ds(row * LEAVES, LEAVES)] = value[
                    :, half * 128 : half * 128 + 128
                ]

    def gathered(leaf, parts):
        return jnp.concatenate(
            [features[part, pl.ds(leaf, DEPTH, stride=LEAVES), :] for part in parts], axis=1
        )

    def source_features(block):
        x, y, z = (geom[block, d].astype(f32) for d in range(3))
        nx, ny, nz = (kernel_scale * geom[block, 3 + d].astype(f32) for d in range(3))
        square = x * x + y * y + z * z + soften_square
        along = nx * x + ny * y + nz * z
        for d, value in enumerate((nx, ny, nz, along)):
            rows[d, pl.ds(block * LEAVES, LEAVES)] = value
        sh, sm, sl = split3(square)
        ah, am, al = split3(-along)
        xh, xm, xl = split3(nx)
        yh, ym, yl = split3(ny)
        zh, zm, zl = split3(nz)
        for row, (first, second) in enumerate((
            (-2.0 * x, xh), (-2.0 * y, yh), (-2.0 * z, zh), (sh, ah), (sm, am), (sl, al),
            (one, zero), (one, zero), (one, zero), (zero, xm), (zero, ym), (zero, zm),
            (zero, xl), (zero, yl), (zero, zl), (zero, zero),
        )):
            put(row, first, second)

        def one_leaf(leaf, _):
            sources[block * LEAVES + leaf] = gathered(leaf, range(4)).astype(bf16)
            return 0

        lax.fori_loop(0, LEAVES, one_leaf, 0, unroll=4)

    source_features(1)

    wants[c] = wants_own[...]
    pltpu.make_async_remote_copy(
        src_ref=wants.at[pl.ds(0, COLS - 1)],
        dst_ref=wants.at[pl.ds(0, COLS - 1)],
        send_sem=want_send,
        recv_sem=want_recv,
        device_id=(g, above),
        device_id_type=MESH,
    ).wait_recv()

    read_wants = load(wants, asked, small_sem.at[3])
    read_wants.wait()

    def answer(d, _):
        peer = lax.rem(c + d, COLS)
        for slot in range(SLOTS):
            outgoing[SLOTS * peer + slot] = skel[asked[peer, slot, c]]
        pltpu.make_async_remote_copy(
            src_ref=outgoing.at[pl.ds(SLOTS * peer, SLOTS)],
            dst_ref=received.at[pl.ds(SLOTS * c, SLOTS)],
            send_sem=far_send,
            recv_sem=far_recv,
            device_id=(g, peer),
            device_id_type=MESH,
        ).start()
        return 0

    lax.fori_loop(1, COLS, answer, 0)
    for slot in range(SLOTS):
        received[SLOTS * c + slot] = skel[asked[c, slot, c]]

    for copy in halo:
        copy.wait_recv()
    source_features(0)
    source_features(2)

    load_nlist.wait()
    px, py, pz = (geom[1, d].astype(f32) for d in range(3))
    th, tm, tl = split3(px * px + py * py + pz * pz)
    for row, value in enumerate(
        (px, py, pz, one, one, one, th, tm, tl, px, py, pz, px, py, pz, zero)
    ):
        put(row, value, zero)

    def near_leaf(leaf, _):
        target = gathered(leaf, range(2)).T
        for d in range(3):
            columns[d] = jnp.broadcast_to(target[:VECTOR_ROWS, d : d + 1], (VECTOR_ROWS, 128))
        target = target.astype(bf16)

        def geometry(q):
            source = sources[q]
            square = jnp.dot(target, source[:, :LEAF], preferred_element_type=f32)
            row = [rows[d, pl.ds(q, 1), :] for d in range(4)]
            parts = []
            for start in range(0, LEAF, 128):
                nx, ny, nz, along = (value[:, start : start + 128] for value in row)
                parts.append(columns[0] * nx + columns[1] * ny + columns[2] * nz - along)
            normal = jnp.concatenate(parts, axis=1)
            rest = jnp.dot(target[VECTOR_ROWS:], source[:, LEAF:], preferred_element_type=f32)
            return square, jnp.concatenate([normal, rest], axis=0)

        total = jnp.zeros((RHS, LEAF), f32)
        held = geometry(nlist[leaf, 0])
        for entry in range(NEAR):
            q = nlist[leaf, entry]
            square, normal = held
            if entry < NEAR - 1:
                held = geometry(nlist[leaf, entry + 1])
            inverse = lax.rsqrt(square)
            tile = ((normal * inverse) * (inverse * inverse)).astype(bf16)
            total = total + lax.dot_general(
                dens[q // LEAVES, q % LEAVES], tile, CONTRACT_LAST, preferred_element_type=f32
            )
        result[leaf] = total
        return 0

    lax.fori_loop(0, LEAVES, near_leaf, 0)

    load_coarse.wait()
    pltpu.make_async_remote_copy(
        src_ref=sums.at[pl.ds(0, ROWS - 1)],
        dst_ref=sums.at[pl.ds(0, ROWS - 1)],
        send_sem=sum_send,
        recv_sem=sum_recv,
        device_id=(lax.rem(g + 1, ROWS), c),
        device_id_type=MESH,
    ).wait_recv()
    siblings = []
    for level in range(LEVELS):
        width = 2**level
        block = g // width
        first = (block + 1 - 2 * lax.rem(block, 2)) * width
        value = sums[first]
        for other in range(1, width):
            value = value + sums[first + other]
        siblings.append(value)
    mixed = jnp.concatenate(
        [
            jnp.concatenate([value[:, :RANK] for value in siblings], axis=1),
            jnp.concatenate([value[:, RANK:] for value in siblings], axis=1),
        ],
        axis=0,
    )
    pieces = jnp.concatenate(split3(mixed), axis=0).astype(bf16)
    products = jnp.dot(
        pieces, coarse_coup[...].reshape(LEVELS * RANK, RANK), preferred_element_type=f32
    )
    field = ((products[2 * RHS :] + products[RHS : 2 * RHS]) + products[:RHS]).astype(bf16)

    load_flist.wait()
    load_fcount.wait()
    load_coup.wait()
    load_down.wait()
    load_tbasis.wait()
    pltpu.make_async_remote_copy(
        src_ref=received.at[pl.ds(0, SLOTS * (COLS - 1))],
        dst_ref=received.at[pl.ds(0, SLOTS * (COLS - 1))],
        send_sem=far_send,
        recv_sem=far_recv,
        device_id=(g, above),
        device_id_type=MESH,
    ).wait_recv()

    def far_leaf(leaf, _):
        count = fcount[leaf]
        upper, lower = [], []
        for entry in range(FAR):
            value = received[flist[entry, leaf]].astype(f32)
            value = jnp.where(entry < count, value, jnp.zeros_like(value))
            upper.append(value[:, :RANK])
            lower.append(value[:, RANK:])
        chosen = jnp.concatenate(
            [jnp.concatenate(upper, axis=1), jnp.concatenate(lower, axis=1)], axis=0
        ).astype(bf16)
        coeff = jnp.dot(
            chosen, coup[leaf].reshape(FAR * RANK, RANK), preferred_element_type=f32
        ) + jnp.dot(field, down[leaf], preferred_element_type=f32)
        result[leaf] = result[leaf] + jnp.dot(
            coeff.astype(bf16), tbasis[leaf], preferred_element_type=f32
        )
        return 0

    lax.fori_loop(0, LEAVES, far_leaf, 0, unroll=4)
    store = pltpu.make_async_copy(result, out, out_sem)
    store.start()

    for copy in halo:
        copy.wait_send()
    pltpu.make_async_remote_copy(
        src_ref=received.at[pl.ds(0, SLOTS * (COLS - 1))],
        dst_ref=received.at[pl.ds(0, SLOTS * (COLS - 1))],
        send_sem=far_send,
        recv_sem=far_recv,
        device_id=(g, above),
        device_id_type=MESH,
    ).wait_send()
    pltpu.make_async_remote_copy(
        src_ref=sums.at[pl.ds(0, ROWS - 1)],
        dst_ref=sums.at[pl.ds(0, ROWS - 1)],
        send_sem=sum_send,
        recv_sem=sum_recv,
        device_id=(lax.rem(g + 1, ROWS), c),
        device_id_type=MESH,
    ).wait_send()

    def sent_want(d, _):
        pltpu.make_async_remote_copy(
            src_ref=wants_own,
            dst_ref=wants.at[c],
            send_sem=want_send,
            recv_sem=want_recv,
            device_id=(g, above),
            device_id_type=MESH,
        ).wait_send()
        return 0

    lax.fori_loop(1, COLS, sent_want, 0)
    store.wait()


def local(
    densities, points, normals, source_basis, target_basis, upward, downward, couplings,
    coarse_couplings, near_list, far_want, far_list, far_count,
):
    anywhere = pl.BlockSpec(memory_space=pl.ANY)
    dma = pltpu.SemaphoreType.DMA
    return pl.pallas_call(
        kernel,
        out_shape=jax.ShapeDtypeStruct((LEAVES, RHS, LEAF), f32),
        in_specs=[anywhere] * 13,
        out_specs=anywhere,
        scratch_shapes=[
            pltpu.VMEM((3, LEAVES, RHS, LEAF), bf16),
            pltpu.VMEM((3, 6, LEAVES, LEAF), bf16),
            pltpu.VMEM((SLOTS, COLS), jnp.int32),
            pltpu.VMEM((COLS, SLOTS, COLS), jnp.int32),
            pltpu.SMEM((COLS, SLOTS, COLS), jnp.int32),
            pltpu.VMEM((LEAVES, RANK, LEAF), bf16),
            pltpu.VMEM((LEAVES, RANK, LEAF), bf16),
            pltpu.VMEM((LEAVES, RANK, RANK), bf16),
            pltpu.VMEM((LEAVES, RANK, RANK), bf16),
            pltpu.VMEM((LEAVES, FAR, RANK, RANK), bf16),
            pltpu.VMEM((LEVELS, RANK, RANK), bf16),
            pltpu.SMEM((LEAVES, NEAR), jnp.int32),
            pltpu.SMEM((FAR, LEAVES), jnp.int32),
            pltpu.SMEM((LEAVES,), jnp.int32),
            pltpu.VMEM((LEAVES, 16, 128), bf16),
            pltpu.VMEM((SLOTS * COLS, 16, 128), bf16),
            pltpu.VMEM((SLOTS * COLS, 16, 128), bf16),
            pltpu.VMEM((ROWS, 16, 128), f32),
            pltpu.VMEM((4, DEPTH * LEAVES, 128), f32),
            pltpu.VMEM((3 * LEAVES, DEPTH, 2 * LEAF), bf16),
            pltpu.VMEM((4, 3 * LEAVES, LEAF), f32),
            pltpu.VMEM((3, VECTOR_ROWS, 128), f32),
            pltpu.VMEM((LEAVES, RHS, LEAF), f32),
            dma((10,)), dma((4,)), dma((4,)), dma((4,)), dma, dma, dma, dma, dma, dma, dma,
        ],
        compiler_params=pltpu.CompilerParams(
            collective_id=0, has_side_effects=True, vmem_limit_bytes=60 * 2**20
        ),
        cost_estimate=pl.CostEstimate(
            flops=2 * 16 * 12 * 65536 * 48, bytes_accessed=6 * 2**20, transcendentals=16 * 12 * 65536
        ),
        name="h2_product",
    )(
        densities,
        points.transpose(1, 0, 2),
        normals.transpose(1, 0, 2),
        source_basis,
        target_basis,
        upward,
        downward,
        couplings,
        coarse_couplings.reshape(LEVELS, RANK, RANK),
        near_list,
        far_want.reshape(COLS, SLOTS).T,
        far_list.T,
        far_count,
    )


def solution(mesh):
    leaf = P(("row", "col"), None, None)
    placed = (
        (leaf,) * 7
        + (P(("row", "col"), None, None, None), P("row", "col", None, None, None))
        + (P(("row", "col"), None), P("row", "col", None, None))
        + (P(("row", "col"), None), P(("row", "col")))
    )
    return jax.shard_map(local, mesh=mesh, in_specs=placed, out_specs=leaf, check_vma=False)
```

time: 193 us -> 64.3 us (0.33); the launches traced: 190 us -> 64.1 us
  Pallas kernels: 0 us -> 62.2 us
  matrix products: 59 us -> 0 us
  starting transfers between devices: 59 us -> 0 us
  other arithmetic: 43.1 us -> 0 us
  local copies, waits for them, and re-layouts: 20.9 us -> 1.88 us
  waiting for transfers between devices: 6.73 us -> 0 us
    pallas_call x0 -> x1, Pallas kernels: none -> 62.2 us  [local(): pl.pallas_call(kernel, out_shape=jax.ShapeDtypeStruct((LEAVES, RHS, LEAF)...]
    dot_general x24 -> x0, matrix products: 59 us -> none  [the longest x16 51.9 us: near_leaf(): jnp.einsum('krq,kqp->rp', sources[:, :rhs_count], kernel_tile, preferred_...]
    ppermute x6 -> x0, starting transfers between devices: 45.8 us -> none  [the longest x4 27.9 us: partner_2(): return lax.ppermute(block, axis, route)]
    select_n x35 -> x0, other arithmetic: 14.9 us -> none  [the longest x32 12.5 us: near_leaf(): sources = jnp.take(padded, source_ids, axis=0)]
    gather x20 -> x0, local copies, waits for them, and re-layouts: 14.1 us -> none  [the longest x16 9 us: near_leaf(): sources = jnp.take(padded, source_ids, axis=0)]
    all_to_all x2 -> x0, starting transfers between devices: 13.2 us -> none  [the longest x1 6.9 us: local(): lax.all_to_all(far_want, 'col', split_axis=2, concat_axis=2, tiled=True)]
    convert_element_type x32 -> x0, other arithmetic: 11.8 us -> none  [the longest x16 11.5 us: near_tile(): target = target_points.astype(jnp.float32)]
    and x18 -> x0, other arithmetic: 11.3 us -> none  [the longest x16 11.3 us: near_leaf(): sources = jnp.take(padded, source_ids, axis=0)]
  transfers between devices with their start and end apart: 8 -> 0, of which waited for: 3 -> 0; matrix products, arithmetic and copies ran while one was open for 58% -> 0% of each run, Pallas kernels for 0% -> 0%
where the time goes in v1:
time: 64.3 us; the launch traced here: 64.1 us
  Pallas kernels  62.2 us (97%)
  local copies, waits for them, and re-layouts  1.88 us (3%)
    pallas_call x1, Pallas kernels, local(): pl.pallas_call(kernel, out_shape=jax.ShapeDtypeStruct((LEAVES, RHS, LEAF)...  62.2 us
    unnamed x1, local copies, waits for them, and re-layouts  1.88 us

profile of v1, /device:TPU:1, one launch (start us, length us, event | category | flops | bytes accessed | tf_op | source)
XLA Modules:
  0.0 64.1 jit_solution(17872776885204322329)
XLA Ops:
  0.0 62.2 %h2_product.1 = f32[16,32,256]{2,1,0:T(8,128)} custom-call(bf16[16,32,256]{2,1,0:T(8,128)(2,1)} %densities.1, bf16[3,16,256]{2,1,0:T(8,128)(2,1)} %bitcast.8, bf16[3,16,256]{2,1,0:T(8,128)(2,1)} %bitcast.9, bf16[16,64,256]{2,1,0:T(8,128)(2,1)} %source_basis.1, bf16[16,64,256]{2,1,0:T(8,128)(2,1)} %target_basis.1, bf16[16,64,64]{2,1,0:T(8,128)(2,1)} %upward.1, ...), custom_call_target="tpu_custom_call" | custom-call | flops 1207959552 | bytes 6291456 | tf_op jit(solution)/shard_map/h2_product/pallas_call | solution.py:379
  62.2 1.9 %copy.15 = f32[16,32,256]{2,1,0:T(8,128)} copy(f32[16,32,256]{2,1,0:T(8,128)} %h2_product.1) | data formatting | bytes 1048576

commit v2 on v1

--- a/solution.py
+++ b/solution.py
@@ -21,7 +21,9 @@
 ROWS = 16
 COLS = 64
 DEPTH = 16
-VECTOR_ROWS = 192
+SELF_GROUP = 8
+NEAR_GROUP = 4
+VECTOR_ROWS = 128
 
 f32 = jnp.float32
 bf16 = jnp.bfloat16
@@ -36,13 +38,18 @@
     return high, middle, rest - middle
 
 
+def pack(value):
+    return jnp.concatenate([value[:16], value[16:]], axis=1)
+
+
 def kernel(
     densities, points, normals, source_basis, target_basis, upward, downward, couplings,
     coarse_couplings, near_list, far_want, far_list, far_count,
     out,
     dens, geom, wants_own, wants, asked, sbasis, tbasis, up, down, coup, coarse_coup,
-    nlist, flist, fcount, skel, outgoing, received, sums, features, sources, rows, columns, result,
-    load_sem, small_sem, halo_send, halo_recv, want_send, want_recv, far_send, far_recv,
+    nlist, flist, fcount, skel, outgoing, received, sums,
+    features, sources, rows, targets, columns, result,
+    load_sem, halo_send, halo_recv, want_send, want_recv, far_send, far_recv,
     sum_send, sum_recv, out_sem,
 ):
     g = lax.axis_index("row")
@@ -50,28 +57,19 @@
     above = lax.rem(c + 1, COLS)
     below = lax.rem(c + COLS - 1, COLS)
 
-    def load(source, target, sem):
-        copy = pltpu.make_async_copy(source, target, sem)
+    barrier = pltpu.get_barrier_semaphore()
+
+    def load(source, target, place):
+        copy = pltpu.make_async_copy(source, target, load_sem.at[place])
         copy.start()
         return copy
 
-    load_points = load(points, geom.at[1, pl.ds(0, 3)], load_sem.at[0])
-    load_normals = load(normals, geom.at[1, pl.ds(3, 3)], load_sem.at[1])
-    load_dens = load(densities, dens.at[1], load_sem.at[2])
-    load_wants = load(far_want, wants_own, load_sem.at[3])
-    load_sbasis = load(source_basis, sbasis, load_sem.at[4])
-    load_up = load(upward, up, load_sem.at[5])
-    load_nlist = load(near_list, nlist, small_sem.at[0])
-    load_flist = load(far_list, flist, small_sem.at[1])
-    load_fcount = load(far_count, fcount, small_sem.at[2])
-    load_coarse = load(coarse_couplings, coarse_coup, load_sem.at[6])
-    load_coup = load(couplings, coup, load_sem.at[7])
-    load_down = load(downward, down, load_sem.at[8])
-    load_tbasis = load(target_basis, tbasis, load_sem.at[9])
-
-    barrier = pltpu.get_barrier_semaphore()
-
-    def greet_col(d, _):
+    load_points = load(points, geom.at[1, pl.ds(0, 3)], 0)
+    load_normals = load(normals, geom.at[1, pl.ds(3, 3)], 1)
+    load_dens = load(densities, dens.at[1], 2)
+    load_wants = load(far_want, wants_own, 3)
+
+    def greet(d, _):
         pl.semaphore_signal(
             barrier, inc=1, device_id=(g, lax.rem(c + d, COLS)), device_id_type=MESH
         )
@@ -83,8 +81,18 @@
         )
         return 0
 
-    lax.fori_loop(1, COLS, greet_col, 0)
+    lax.fori_loop(1, COLS, greet, 0)
     lax.fori_loop(1, ROWS, greet_row, 0)
+
+    load_sbasis = load(source_basis, sbasis, 4)
+    load_up = load(upward, up, 5)
+    load_nlist = load(near_list, nlist, 6)
+    load_flist = load(far_list, flist, 7)
+    load_fcount = load(far_count, fcount, 8)
+    load_coup = load(couplings, coup, 9)
+    load_coarse = load(coarse_couplings, coarse_coup, 10)
+    load_down = load(downward, down, 11)
+    load_tbasis = load(target_basis, tbasis, 12)
 
     load_points.wait()
     load_normals.wait()
@@ -122,17 +130,15 @@
 
     load_sbasis.wait()
     load_up.wait()
-
     total = jnp.zeros((RHS, RANK), f32)
     for leaf in range(LEAVES):
         value = lax.dot_general(
             dens[1, leaf], sbasis[leaf], CONTRACT_LAST, preferred_element_type=f32
         )
         rounded = value.astype(bf16)
-        value = rounded.astype(f32)
-        skel[leaf] = jnp.concatenate([value[:16], value[16:]], axis=1).astype(bf16)
+        skel[leaf] = pack(rounded.astype(f32)).astype(bf16)
         total = total + jnp.dot(rounded, up[leaf], preferred_element_type=f32)
-    sums[g] = jnp.concatenate([total[:16], total[16:]], axis=1)
+    sums[g] = pack(total)
 
     def send_sum(d, _):
         pltpu.make_async_remote_copy(
@@ -188,18 +194,75 @@
         lax.fori_loop(0, LEAVES, one_leaf, 0, unroll=4)
 
     source_features(1)
+    px, py, pz = (geom[1, d].astype(f32) for d in range(3))
+    th, tm, tl = split3(px * px + py * py + pz * pz)
+    for row, value in enumerate(
+        (px, py, pz, one, one, one, th, tm, tl, px, py, pz, px, py, pz, zero)
+    ):
+        put(row, value, zero)
+
+    def target_features(leaf, _):
+        target = gathered(leaf, range(2)).T
+        for d in range(3):
+            columns[leaf, d] = jnp.broadcast_to(
+                target[:VECTOR_ROWS, d : d + 1], (VECTOR_ROWS, 128)
+            )
+        targets[leaf] = target.astype(bf16)
+        return 0
+
+    lax.fori_loop(0, LEAVES, target_features, 0, unroll=2)
+
+    def geometry(leaf, q):
+        source = sources[q]
+        target = targets[leaf]
+        square = jnp.dot(target, source[:, :LEAF], preferred_element_type=f32)
+        row = [rows[d, pl.ds(q, 1), :] for d in range(4)]
+        column = [columns[leaf, d] for d in range(3)]
+        parts = []
+        for start in range(0, LEAF, 128):
+            nx, ny, nz, along = (value[:, start : start + 128] for value in row)
+            parts.append(column[0] * nx + column[1] * ny + column[2] * nz - along)
+        normal = jnp.concatenate(parts, axis=1)
+        rest = jnp.dot(target[VECTOR_ROWS:], source[:, LEAF:], preferred_element_type=f32)
+        return square, jnp.concatenate([normal, rest], axis=0)
+
+    def tile(square, normal):
+        inverse = lax.rsqrt(square)
+        return ((normal * inverse) * (inverse * inverse)).astype(bf16)
+
+    def product(q, formed):
+        return lax.dot_general(
+            dens[q // LEAVES, q % LEAVES], formed, CONTRACT_LAST, preferred_element_type=f32
+        )
+
+    def near_self(group, _):
+        first = group * SELF_GROUP
+        held = geometry(first, LEAVES + first)
+        for place in range(SELF_GROUP):
+            leaf = first + place
+            square, normal = held
+            if place < SELF_GROUP - 1:
+                held = geometry(leaf + 1, LEAVES + leaf + 1)
+            result[leaf] = product(LEAVES + leaf, tile(square, normal))
+        return 0
+
+    lax.fori_loop(0, LEAVES // SELF_GROUP, near_self, 0)
 
     wants[c] = wants_own[...]
-    pltpu.make_async_remote_copy(
+    requests = pltpu.make_async_remote_copy(
         src_ref=wants.at[pl.ds(0, COLS - 1)],
         dst_ref=wants.at[pl.ds(0, COLS - 1)],
         send_sem=want_send,
         recv_sem=want_recv,
         device_id=(g, above),
         device_id_type=MESH,
-    ).wait_recv()
-
-    read_wants = load(wants, asked, small_sem.at[3])
+    )
+    requests.wait_recv()
+    read_wants = load(wants, asked, 13)
+    halo[0].wait_recv()
+    halo[1].wait_recv()
+    source_features(0)
+    source_features(2)
     read_wants.wait()
 
     def answer(d, _):
@@ -220,63 +283,43 @@
     for slot in range(SLOTS):
         received[SLOTS * c + slot] = skel[asked[c, slot, c]]
 
-    for copy in halo:
-        copy.wait_recv()
-    source_features(0)
-    source_features(2)
-
+    halo[2].wait_recv()
+    halo[3].wait_recv()
     load_nlist.wait()
-    px, py, pz = (geom[1, d].astype(f32) for d in range(3))
-    th, tm, tl = split3(px * px + py * py + pz * pz)
-    for row, value in enumerate(
-        (px, py, pz, one, one, one, th, tm, tl, px, py, pz, px, py, pz, zero)
-    ):
-        put(row, value, zero)
-
-    def near_leaf(leaf, _):
-        target = gathered(leaf, range(2)).T
-        for d in range(3):
-            columns[d] = jnp.broadcast_to(target[:VECTOR_ROWS, d : d + 1], (VECTOR_ROWS, 128))
-        target = target.astype(bf16)
-
-        def geometry(q):
-            source = sources[q]
-            square = jnp.dot(target, source[:, :LEAF], preferred_element_type=f32)
-            row = [rows[d, pl.ds(q, 1), :] for d in range(4)]
-            parts = []
-            for start in range(0, LEAF, 128):
-                nx, ny, nz, along = (value[:, start : start + 128] for value in row)
-                parts.append(columns[0] * nx + columns[1] * ny + columns[2] * nz - along)
-            normal = jnp.concatenate(parts, axis=1)
-            rest = jnp.dot(target[VECTOR_ROWS:], source[:, LEAF:], preferred_element_type=f32)
-            return square, jnp.concatenate([normal, rest], axis=0)
-
-        total = jnp.zeros((RHS, LEAF), f32)
-        held = geometry(nlist[leaf, 0])
-        for entry in range(NEAR):
-            q = nlist[leaf, entry]
-            square, normal = held
-            if entry < NEAR - 1:
-                held = geometry(nlist[leaf, entry + 1])
-            inverse = lax.rsqrt(square)
-            tile = ((normal * inverse) * (inverse * inverse)).astype(bf16)
-            total = total + lax.dot_general(
-                dens[q // LEAVES, q % LEAVES], tile, CONTRACT_LAST, preferred_element_type=f32
-            )
-        result[leaf] = total
-        return 0
-
-    lax.fori_loop(0, LEAVES, near_leaf, 0)
+
+    def near_leaves(step, _):
+        first = step * NEAR_GROUP
+        work = [(place, entry) for place in range(NEAR_GROUP) for entry in range(1, NEAR)]
+        totals = [result[first + place] for place in range(NEAR_GROUP)]
+        held = geometry(first, nlist[first, 1])
+        formed = None
+        for number in range(len(work) + 1):
+            if number < len(work):
+                square, normal = held
+            if number + 1 < len(work):
+                place, entry = work[number + 1]
+                held = geometry(first + place, nlist[first + place, entry])
+            if number:
+                place, entry = work[number - 1]
+                totals[place] = totals[place] + product(nlist[first + place, entry], formed)
+            if number < len(work):
+                formed = tile(square, normal)
+        for place in range(NEAR_GROUP):
+            result[first + place] = totals[place]
+        return 0
+
+    lax.fori_loop(0, LEAVES // NEAR_GROUP, near_leaves, 0)
 
     load_coarse.wait()
-    pltpu.make_async_remote_copy(
+    row_sums = pltpu.make_async_remote_copy(
         src_ref=sums.at[pl.ds(0, ROWS - 1)],
         dst_ref=sums.at[pl.ds(0, ROWS - 1)],
         send_sem=sum_send,
         recv_sem=sum_recv,
         device_id=(lax.rem(g + 1, ROWS), c),
         device_id_type=MESH,
-    ).wait_recv()
+    )
+    row_sums.wait_recv()
     siblings = []
     for level in range(LEVELS):
         width = 2**level
@@ -299,19 +342,20 @@
     )
     field = ((products[2 * RHS :] + products[RHS : 2 * RHS]) + products[:RHS]).astype(bf16)
 
+    load_down.wait()
+    load_tbasis.wait()
     load_flist.wait()
     load_fcount.wait()
     load_coup.wait()
-    load_down.wait()
-    load_tbasis.wait()
-    pltpu.make_async_remote_copy(
+    arrivals = pltpu.make_async_remote_copy(
         src_ref=received.at[pl.ds(0, SLOTS * (COLS - 1))],
         dst_ref=received.at[pl.ds(0, SLOTS * (COLS - 1))],
         send_sem=far_send,
         recv_sem=far_recv,
         device_id=(g, above),
         device_id_type=MESH,
-    ).wait_recv()
+    )
+    arrivals.wait_recv()
 
     def far_leaf(leaf, _):
         count = fcount[leaf]
@@ -338,35 +382,10 @@
 
     for copy in halo:
         copy.wait_send()
-    pltpu.make_async_remote_copy(
-        src_ref=received.at[pl.ds(0, SLOTS * (COLS - 1))],
-        dst_ref=received.at[pl.ds(0, SLOTS * (COLS - 1))],
-        send_sem=far_send,
-        recv_sem=far_recv,
-        device_id=(g, above),
-        device_id_type=MESH,
-    ).wait_send()
-    pltpu.make_async_remote_copy(
-        src_ref=sums.at[pl.ds(0, ROWS - 1)],
-        dst_ref=sums.at[pl.ds(0, ROWS - 1)],
-        send_sem=sum_send,
-        recv_sem=sum_recv,
-        device_id=(lax.rem(g + 1, ROWS), c),
-        device_id_type=MESH,
-    ).wait_send()
-
-    def sent_want(d, _):
-        pltpu.make_async_remote_copy(
-            src_ref=wants_own,
-            dst_ref=wants.at[c],
-            send_sem=want_send,
-            recv_sem=want_recv,
-            device_id=(g, above),
-            device_id_type=MESH,
-        ).wait_send()
-        return 0
-
-    lax.fori_loop(1, COLS, sent_want, 0)
+    arrivals.wait_send()
+
+    requests.wait_send()
+    row_sums.wait_send()
     store.wait()
 
 
@@ -403,15 +422,16 @@
             pltpu.VMEM((4, DEPTH * LEAVES, 128), f32),
             pltpu.VMEM((3 * LEAVES, DEPTH, 2 * LEAF), bf16),
             pltpu.VMEM((4, 3 * LEAVES, LEAF), f32),
-            pltpu.VMEM((3, VECTOR_ROWS, 128), f32),
+            pltpu.VMEM((LEAVES, LEAF, DEPTH), bf16),
+            pltpu.VMEM((LEAVES, 3, VECTOR_ROWS, 128), f32),
             pltpu.VMEM((LEAVES, RHS, LEAF), f32),
-            dma((10,)), dma((4,)), dma((4,)), dma((4,)), dma, dma, dma, dma, dma, dma, dma,
+            dma((14,)), dma((4,)), dma((4,)), dma, dma, dma, dma, dma, dma, dma,
         ],
         compiler_params=pltpu.CompilerParams(
             collective_id=0, has_side_effects=True, vmem_limit_bytes=60 * 2**20
         ),
         cost_estimate=pl.CostEstimate(
-            flops=2 * 16 * 12 * 65536 * 48, bytes_accessed=6 * 2**20, transcendentals=16 * 12 * 65536
+            flops=2 * 16 * 12 * 65536 * 192, bytes_accessed=6 * 2**20, transcendentals=16 * 12 * 65536
         ),
         name="h2_product",
     )(

time: 64.3 us -> 57.3 us (0.89)
  Pallas kernels: 62.2 us -> 55.2 us
    pallas_call x1, Pallas kernels: 62.2 us -> 55.2 us  [local(): pl.pallas_call(kernel, out_shape=jax.ShapeDtypeStruct((LEAVES, RHS, LEAF)...]
where the time goes in v2:
time: 57.3 us; the launch traced here: 57.1 us
  Pallas kernels  55.2 us (96%)
  local copies, waits for them, and re-layouts  1.88 us (3%)
    pallas_call x1, Pallas kernels, local(): pl.pallas_call(kernel, out_shape=jax.ShapeDtypeStruct((LEAVES, RHS, LEAF)...  55.2 us
    unnamed x1, local copies, waits for them, and re-layouts  1.88 us

profile of v2, /device:TPU:1, one launch (start us, length us, event | category | flops | bytes accessed | tf_op | source)
XLA Modules:
  0.0 57.1 jit_solution(16897564026432269145)
XLA Ops:
  0.0 55.2 %h2_product.1 = f32[16,32,256]{2,1,0:T(8,128)} custom-call(bf16[16,32,256]{2,1,0:T(8,128)(2,1)} %densities.1, bf16[3,16,256]{2,1,0:T(8,128)(2,1)} %bitcast.8, bf16[3,16,256]{2,1,0:T(8,128)(2,1)} %bitcast.9, bf16[16,64,256]{2,1,0:T(8,128)(2,1)} %source_basis.1, bf16[16,64,256]{2,1,0:T(8,128)(2,1)} %target_basis.1, bf16[16,64,64]{2,1,0:T(8,128)(2,1)} %upward.1, ...), custom_call_target="tpu_custom_call" | custom-call | flops 4831838208 | bytes 6291456 | tf_op jit(solution)/shard_map/h2_product/pallas_call | solution.py:398
  55.2 1.9 %copy.15 = f32[16,32,256]{2,1,0:T(8,128)} copy(f32[16,32,256]{2,1,0:T(8,128)} %h2_product.1) | data formatting | bytes 1048576

commit v3 on v2

--- a/solution.py
+++ b/solution.py
@@ -20,6 +20,8 @@
 LEVELS = 4
 ROWS = 16
 COLS = 64
+PEER_GROUP = 7
+PEER_GROUPS = (COLS - 1) // PEER_GROUP
 DEPTH = 16
 SELF_GROUP = 8
 NEAR_GROUP = 4
@@ -46,10 +48,10 @@
     densities, points, normals, source_basis, target_basis, upward, downward, couplings,
     coarse_couplings, near_list, far_want, far_list, far_count,
     out,
-    dens, geom, wants_own, wants, asked, sbasis, tbasis, up, down, coup, coarse_coup,
+    dens, geom, wants_own, wants, asked_own, asked, sbasis, tbasis, up, down, coup, coarse_coup,
     nlist, flist, fcount, skel, outgoing, received, sums,
     features, sources, rows, targets, columns, result,
-    load_sem, halo_send, halo_recv, want_send, want_recv, far_send, far_recv,
+    load_sem, read_sem, halo_send, halo_recv, want_send, want_recv, far_send, far_recv,
     sum_send, sum_recv, out_sem,
 ):
     g = lax.axis_index("row")
@@ -68,6 +70,18 @@
     load_normals = load(normals, geom.at[1, pl.ds(3, 3)], 1)
     load_dens = load(densities, dens.at[1], 2)
     load_wants = load(far_want, wants_own, 3)
+    load_asked = load(far_want, asked_own, 13)
+
+    def offset(number):
+        return COLS // 2 + ((number + 1) // 2) * (1 - 2 * lax.rem(number, 2))
+
+    def each_group(act):
+        def one_group(group, _):
+            for place in range(PEER_GROUP):
+                act(group, group * PEER_GROUP + place)
+            return 0
+
+        lax.fori_loop(0, PEER_GROUPS, one_group, 0)
 
     def greet(d, _):
         pl.semaphore_signal(
@@ -97,8 +111,33 @@
     load_points.wait()
     load_normals.wait()
     load_dens.wait()
+
+    load_sbasis.wait()
+    load_up.wait()
+    total = jnp.zeros((RHS, RANK), f32)
+    for leaf in range(LEAVES):
+        value = lax.dot_general(
+            dens[1, leaf], sbasis[leaf], CONTRACT_LAST, preferred_element_type=f32
+        )
+        rounded = value.astype(bf16)
+        skel[leaf] = pack(rounded.astype(f32)).astype(bf16)
+        total = total + jnp.dot(rounded, up[leaf], preferred_element_type=f32)
+    sums[g] = pack(total)
+
     load_wants.wait()
     pl.semaphore_wait(barrier, COLS + ROWS - 2)
+
+    def send_want(group, number):
+        pltpu.make_async_remote_copy(
+            src_ref=wants_own,
+            dst_ref=wants.at[number],
+            send_sem=want_send,
+            recv_sem=want_recv.at[group],
+            device_id=(g, lax.rem(c + offset(number), COLS)),
+            device_id_type=MESH,
+        ).start()
+
+    each_group(send_want)
 
     halo = []
     for index, (buffer, slot, target) in enumerate(
@@ -114,31 +153,6 @@
         )
         copy.start()
         halo.append(copy)
-
-    def send_want(d, _):
-        pltpu.make_async_remote_copy(
-            src_ref=wants_own,
-            dst_ref=wants.at[c],
-            send_sem=want_send,
-            recv_sem=want_recv,
-            device_id=(g, lax.rem(c + d, COLS)),
-            device_id_type=MESH,
-        ).start()
-        return 0
-
-    lax.fori_loop(1, COLS, send_want, 0)
-
-    load_sbasis.wait()
-    load_up.wait()
-    total = jnp.zeros((RHS, RANK), f32)
-    for leaf in range(LEAVES):
-        value = lax.dot_general(
-            dens[1, leaf], sbasis[leaf], CONTRACT_LAST, preferred_element_type=f32
-        )
-        rounded = value.astype(bf16)
-        skel[leaf] = pack(rounded.astype(f32)).astype(bf16)
-        total = total + jnp.dot(rounded, up[leaf], preferred_element_type=f32)
-    sums[g] = pack(total)
 
     def send_sum(d, _):
         pltpu.make_async_remote_copy(
@@ -210,7 +224,7 @@
         targets[leaf] = target.astype(bf16)
         return 0
 
-    lax.fori_loop(0, LEAVES, target_features, 0, unroll=2)
+    lax.fori_loop(0, LEAVES, target_features, 0, unroll=8)
 
     def geometry(leaf, q):
         source = sources[q]
@@ -248,41 +262,56 @@
 
     lax.fori_loop(0, LEAVES // SELF_GROUP, near_self, 0)
 
-    wants[c] = wants_own[...]
-    requests = pltpu.make_async_remote_copy(
-        src_ref=wants.at[pl.ds(0, COLS - 1)],
-        dst_ref=wants.at[pl.ds(0, COLS - 1)],
-        send_sem=want_send,
-        recv_sem=want_recv,
-        device_id=(g, above),
-        device_id_type=MESH,
-    )
-    requests.wait_recv()
-    read_wants = load(wants, asked, 13)
+    load_asked.wait()
+
+    def read_group(group):
+        chosen = pl.ds(group * PEER_GROUP, PEER_GROUP)
+        return pltpu.make_async_copy(wants.at[chosen], asked.at[chosen], read_sem.at[group])
+
+    def fetch(group):
+        chosen = pl.ds(group * PEER_GROUP, PEER_GROUP)
+        pltpu.make_async_remote_copy(
+            src_ref=wants.at[chosen],
+            dst_ref=wants.at[chosen],
+            send_sem=want_send,
+            recv_sem=want_recv.at[group],
+            device_id=(g, above),
+            device_id_type=MESH,
+        ).wait_recv()
+        read_group(group).start()
+
+    def answer(group):
+        read_group(group).wait()
+        for place in range(PEER_GROUP):
+            number = group * PEER_GROUP + place
+            for slot in range(SLOTS):
+                outgoing[SLOTS * number + slot] = skel[asked[number, slot, c]]
+            pltpu.make_async_remote_copy(
+                src_ref=outgoing.at[pl.ds(SLOTS * number, SLOTS)],
+                dst_ref=received.at[pl.ds(SLOTS * c, SLOTS)],
+                send_sem=far_send,
+                recv_sem=far_recv,
+                device_id=(g, lax.rem(c + COLS - offset(number), COLS)),
+                device_id_type=MESH,
+            ).start()
+
+    def fetch_one(group, _):
+        fetch(group)
+        return 0
+
+    def answer_one(group, _):
+        answer(group)
+        return 0
+
+    lax.fori_loop(0, PEER_GROUPS, fetch_one, 0)
+    lax.fori_loop(0, PEER_GROUPS, answer_one, 0)
+    for slot in range(SLOTS):
+        received[SLOTS * c + slot] = skel[asked_own[slot, c]]
+
     halo[0].wait_recv()
     halo[1].wait_recv()
     source_features(0)
     source_features(2)
-    read_wants.wait()
-
-    def answer(d, _):
-        peer = lax.rem(c + d, COLS)
-        for slot in range(SLOTS):
-            outgoing[SLOTS * peer + slot] = skel[asked[peer, slot, c]]
-        pltpu.make_async_remote_copy(
-            src_ref=outgoing.at[pl.ds(SLOTS * peer, SLOTS)],
-            dst_ref=received.at[pl.ds(SLOTS * c, SLOTS)],
-            send_sem=far_send,
-            recv_sem=far_recv,
-            device_id=(g, peer),
-            device_id_type=MESH,
-        ).start()
-        return 0
-
-    lax.fori_loop(1, COLS, answer, 0)
-    for slot in range(SLOTS):
-        received[SLOTS * c + slot] = skel[asked[c, slot, c]]
-
     halo[2].wait_recv()
     halo[3].wait_recv()
     load_nlist.wait()
@@ -376,7 +405,7 @@
         )
         return 0
 
-    lax.fori_loop(0, LEAVES, far_leaf, 0, unroll=4)
+    lax.fori_loop(0, LEAVES, far_leaf, 0, unroll=8)
     store = pltpu.make_async_copy(result, out, out_sem)
     store.start()
 
@@ -384,7 +413,14 @@
         copy.wait_send()
     arrivals.wait_send()
 
-    requests.wait_send()
+    pltpu.make_async_remote_copy(
+        src_ref=wants.at[pl.ds(0, COLS - 1)],
+        dst_ref=wants.at[pl.ds(0, COLS - 1)],
+        send_sem=want_send,
+        recv_sem=want_recv.at[0],
+        device_id=(g, above),
+        device_id_type=MESH,
+    ).wait_send()
     row_sums.wait_send()
     store.wait()
 
@@ -404,8 +440,9 @@
             pltpu.VMEM((3, LEAVES, RHS, LEAF), bf16),
             pltpu.VMEM((3, 6, LEAVES, LEAF), bf16),
             pltpu.VMEM((SLOTS, COLS), jnp.int32),
-            pltpu.VMEM((COLS, SLOTS, COLS), jnp.int32),
-            pltpu.SMEM((COLS, SLOTS, COLS), jnp.int32),
+            pltpu.VMEM((COLS - 1, SLOTS, COLS), jnp.int32),
+            pltpu.SMEM((SLOTS, COLS), jnp.int32),
+            pltpu.SMEM((COLS - 1, SLOTS, COLS), jnp.int32),
             pltpu.VMEM((LEAVES, RANK, LEAF), bf16),
             pltpu.VMEM((LEAVES, RANK, LEAF), bf16),
             pltpu.VMEM((LEAVES, RANK, RANK), bf16),
@@ -416,7 +453,7 @@
             pltpu.SMEM((FAR, LEAVES), jnp.int32),
             pltpu.SMEM((LEAVES,), jnp.int32),
             pltpu.VMEM((LEAVES, 16, 128), bf16),
-            pltpu.VMEM((SLOTS * COLS, 16, 128), bf16),
+            pltpu.VMEM((SLOTS * (COLS - 1), 16, 128), bf16),
             pltpu.VMEM((SLOTS * COLS, 16, 128), bf16),
             pltpu.VMEM((ROWS, 16, 128), f32),
             pltpu.VMEM((4, DEPTH * LEAVES, 128), f32),
@@ -425,7 +462,8 @@
             pltpu.VMEM((LEAVES, LEAF, DEPTH), bf16),
             pltpu.VMEM((LEAVES, 3, VECTOR_ROWS, 128), f32),
             pltpu.VMEM((LEAVES, RHS, LEAF), f32),
-            dma((14,)), dma((4,)), dma((4,)), dma, dma, dma, dma, dma, dma, dma,
+            dma((14,)), dma((PEER_GROUPS,)), dma((4,)), dma((4,)), dma, dma((PEER_GROUPS,)),
+            dma, dma, dma, dma, dma,
         ],
         compiler_params=pltpu.CompilerParams(
             collective_id=0, has_side_effects=True, vmem_limit_bytes=60 * 2**20

time: 57.3 us -> 53.8 us (0.939)
  Pallas kernels: 55.2 us -> 51.7 us
    pallas_call x1, Pallas kernels: 55.2 us -> 51.7 us  [local(): pl.pallas_call(kernel, out_shape=jax.ShapeDtypeStruct((LEAVES, RHS, LEAF)...]
where the time goes in v3:
time: 53.8 us; the launch traced here: 53.6 us
  Pallas kernels  51.7 us (96%)
  local copies, waits for them, and re-layouts  1.88 us (3%)
    pallas_call x1, Pallas kernels, local(): pl.pallas_call(kernel, out_shape=jax.ShapeDtypeStruct((LEAVES, RHS, LEAF)...  51.7 us
    unnamed x1, local copies, waits for them, and re-layouts  1.88 us

profile of v3, /device:TPU:1, one launch (start us, length us, event | category | flops | bytes accessed | tf_op | source)
XLA Modules:
  0.0 53.6 jit_solution(12447545726417597468)
XLA Ops:
  0.0 51.7 %h2_product.1 = f32[16,32,256]{2,1,0:T(8,128)} custom-call(bf16[16,32,256]{2,1,0:T(8,128)(2,1)} %densities.1, bf16[3,16,256]{2,1,0:T(8,128)(2,1)} %bitcast.8, bf16[3,16,256]{2,1,0:T(8,128)(2,1)} %bitcast.9, bf16[16,64,256]{2,1,0:T(8,128)(2,1)} %source_basis.1, bf16[16,64,256]{2,1,0:T(8,128)(2,1)} %target_basis.1, bf16[16,64,64]{2,1,0:T(8,128)(2,1)} %upward.1, ...), custom_call_target="tpu_custom_call" | custom-call | flops 4831838208 | bytes 6291456 | tf_op jit(solution)/shard_map/h2_product/pallas_call | solution.py:434
  51.7 1.9 %copy.15 = f32[16,32,256]{2,1,0:T(8,128)} copy(f32[16,32,256]{2,1,0:T(8,128)} %h2_product.1) | data formatting | bytes 1048576

commit v4 on v3

--- a/solution.py
+++ b/solution.py
@@ -25,7 +25,7 @@
 DEPTH = 16
 SELF_GROUP = 8
 NEAR_GROUP = 4
-VECTOR_ROWS = 128
+VECTOR_ROWS = 96
 
 f32 = jnp.float32
 bf16 = jnp.bfloat16

time: 53.8 us -> 53.4 us (level)
  no operation moved by 1% of the time
where the time goes in v4:
time: 53.4 us; the launch traced here: 53.2 us
  Pallas kernels  51.3 us (96%)
  local copies, waits for them, and re-layouts  1.88 us (4%)
    pallas_call x1, Pallas kernels, local(): pl.pallas_call(kernel, out_shape=jax.ShapeDtypeStruct((LEAVES, RHS, LEAF)...  51.3 us
    unnamed x1, local copies, waits for them, and re-layouts  1.88 us

profile of v4, /device:TPU:1, one launch (start us, length us, event | category | flops | bytes accessed | tf_op | source)
XLA Modules:
  0.0 53.2 jit_solution(5612491670023541393)
XLA Ops:
  0.0 51.3 %h2_product.1 = f32[16,32,256]{2,1,0:T(8,128)} custom-call(bf16[16,32,256]{2,1,0:T(8,128)(2,1)} %densities.1, bf16[3,16,256]{2,1,0:T(8,128)(2,1)} %bitcast.8, bf16[3,16,256]{2,1,0:T(8,128)(2,1)} %bitcast.9, bf16[16,64,256]{2,1,0:T(8,128)(2,1)} %source_basis.1, bf16[16,64,256]{2,1,0:T(8,128)(2,1)} %target_basis.1, bf16[16,64,64]{2,1,0:T(8,128)(2,1)} %upward.1, ...), custom_call_target="tpu_custom_call" | custom-call | flops 4831838208 | bytes 6291456 | tf_op jit(solution)/shard_map/h2_product/pallas_call | solution.py:434
  51.3 1.9 %copy.15 = f32[16,32,256]{2,1,0:T(8,128)} copy(f32[16,32,256]{2,1,0:T(8,128)} %h2_product.1) | data formatting | bytes 1048576
